TPU v7x, 256 devices: a whole 4x4x8 slice. The times are simulated.
256 devices in a mesh: dom: 64 (over x, z, core), mp: 4 (over y).
Axes of the slice: x: 4, y: 4, z: 8, core: 2. Of those that a mesh axis runs over, the one named last changes fastest.
Arguments:
- features: bfloat16 [262144, 512], P('dom', 'mp'), may hold values from -6 to 6
- history: bfloat16 [262144, 512], P('dom', 'mp'), may hold values from -6 to 6
- weight: bfloat16 [512, 512], P(None, 'mp'), may hold values from -0.25 to 0.25
- bias_vector: float32 [512], P('mp'), may hold values from -3 to 3
- cotangent: bfloat16 [262144, 512], P('dom', 'mp'), may hold values from -6 to 6
- adj_tiles: bfloat16 [12288, 128, 128], P('dom'), may hold values from 0 to 0.071777344
- send_list: int32 [64, 64, 2], P('dom'), may hold values from -1 to 63, as said below
- batch_slot: int32 [64, 32], P('dom'), may hold values from 0 to 126, as said below
- tile_src: int32 [64, 192], P('dom'), may hold values from 0 to 127, as said below
Outputs:
- refreshed: bfloat16 [262144, 512], P('dom', 'mp')
- feat_grad: bfloat16 [262144, 512], P('dom', 'mp')
- weight_grad: float32 [512, 512], P(None, 'mp')
- bias_grad: float32 [512], P('mp')
Inputs may be any that keep to these rules, and one draw needn't show every extreme that they name: send_list[s, c, k] names a block of owner s's table (feature blocks 0..31, then history blocks 32..63) or is -1 for an empty slot. Feature block j of each owner stands in exactly one entry over all c, always in slot 0; slot 1 never holds a feature block. batch_slot[c, j] = s * 2 + j // 64 for the one owner s with send_list[s, c, j // 64] = j. tile_src[c, t] is a slot s * 2 + k with send_list[s, c, k] >= 0; tile t of device c feeds batch block t // 6.
All inputs are finite; a program needn't handle non-finite values.
Results may differ from a plain program's by a relative error of at most 0.012.
Values may be sent and summed in bfloat16 or wider, within the bound.
A program may use at most 128 MiB of HBM per device.

v0:
```python
import jax
import jax.numpy as jnp
from jax import lax
from jax.sharding import PartitionSpec as P


def activate(preact):
    return jax.nn.gelu(preact, approximate=True)


def on_device(
    features, history, weight, bias_vector, cotangent, adj_tiles, send_list, batch_slot, tile_src
):
    rank_count = lax.axis_size("dom")
    block_rows = adj_tiles.shape[1]
    col_share = features.shape[1]
    block_count = features.shape[0] // block_rows
    slot_count = send_list.shape[2]
    lane_count = slot_count - 1
    tiles_per = tile_src.shape[1] // block_count
    own_table = jnp.concatenate(
        [
            features.reshape(block_count, block_rows, col_share),
            history.reshape(block_count, block_rows, col_share),
        ],
        axis=0,
    )
    wanted = send_list[0]
    picked = own_table[jnp.clip(wanted, 0, 2 * block_count - 1)]
    outgoing = jnp.where((wanted >= 0)[:, :, None, None], picked, jnp.zeros_like(picked))
    arrived = lax.all_to_all(outgoing, "dom", split_axis=0, concat_axis=0, tiled=True)
    arrived = arrived.reshape(rank_count * slot_count, block_rows, col_share)
    src_slots = tile_src[0]
    gathered = arrived[src_slots].reshape(block_count, tiles_per, block_rows, col_share)
    tile_vals = adj_tiles.reshape(block_count, tiles_per, block_rows, block_rows)
    mixed = jnp.einsum(
        "jpab,jpbc->jac", tile_vals, gathered, preferred_element_type=jnp.float32
    ).astype(jnp.bfloat16)
    mixed_rows = mixed.reshape(block_count * block_rows, col_share)
    mixed_full = lax.all_gather(mixed_rows, "mp", axis=1, tiled=True)
    preact = jnp.dot(mixed_full, weight, preferred_element_type=jnp.float32) + bias_vector
    fresh_rows, pullback = jax.vjp(activate, preact)
    fresh_blocks = fresh_rows.astype(jnp.bfloat16).reshape(block_count, block_rows, col_share)
    owner_rank = batch_slot[0] // slot_count
    lane_ids = jnp.arange(block_count) // rank_count
    return_ids = wanted[:, :lane_count]
    place_index = jnp.where(
        (return_ids >= 0) & (return_ids < block_count), return_ids, block_count
    ).reshape(-1)

    def pack_out(values):
        empty = jnp.zeros((rank_count, lane_count, block_rows, col_share), jnp.bfloat16)
        return empty.at[owner_rank, lane_ids].set(values)

    def settle(received):
        empty = jnp.zeros((block_count, block_rows, col_share), jnp.bfloat16)
        placed = empty.at[place_index].set(received.reshape(-1, block_rows, col_share), mode="drop")
        return placed.reshape(block_count * block_rows, col_share)

    pre_grad = pullback(cotangent.astype(jnp.float32))[0].astype(jnp.bfloat16)
    weight_part = jnp.einsum("rk,rc->kc", mixed_full, pre_grad, preferred_element_type=jnp.float32)
    bias_part = jnp.sum(pre_grad, axis=0, dtype=jnp.float32)
    weight_total, bias_total = lax.psum((weight_part, bias_part), "dom")
    weight_grad = weight_total / rank_count
    bias_grad = bias_total / rank_count
    partial_terms = jnp.einsum("rc,kc->rk", pre_grad, weight, preferred_element_type=jnp.float32)
    agg_grad = lax.psum_scatter(partial_terms, "mp", scatter_dimension=1, tiled=True).astype(
        jnp.bfloat16
    )
    grad_blocks = agg_grad.reshape(block_count, block_rows, col_share)
    back_terms = jnp.einsum(
        "jpab,jac->jpbc", tile_vals, grad_blocks, preferred_element_type=jnp.float32
    )
    back_terms = back_terms.reshape(block_count * tiles_per, block_rows, col_share)
    hit_table = (src_slots[:, None] == batch_slot[0][None, :]).astype(jnp.float32)
    block_grad = jnp.einsum("tj,tbc->jbc", hit_table, back_terms).astype(jnp.bfloat16)
    back_fresh, back_grad = (
        lax.all_to_all(pack_out(fresh_blocks), "dom", split_axis=0, concat_axis=0, tiled=True),
        lax.all_to_all(pack_out(block_grad), "dom", split_axis=0, concat_axis=0, tiled=True),
    )
    refreshed = settle(back_fresh)
    feat_grad = settle(back_grad)
    return (refreshed, feat_grad, weight_grad, bias_grad)


def solution(mesh):
    placed = (
        P("dom", "mp"),
        P("dom", "mp"),
        P(None, "mp"),
        P("mp"),
        P("dom", "mp"),
        P("dom", None, None),
        P("dom", None, None),
        P("dom", None),
        P("dom", None),
    )
    return jax.shard_map(
        on_device,
        mesh=mesh,
        in_specs=placed,
        out_specs=(P("dom", "mp"), P("dom", "mp"), P(None, "mp"), P("mp")),
        check_vma=False,
    )
```

profile of v0, /device:TPU:1, one launch (start us, length us, event | category | flops | bytes accessed | tf_op | source)
XLA Modules:
  0.0 541.4 jit_solution(13006338078804305021)
XLA Ops:
  7.2 0.0 copy-start
  7.2 0.7 broadcast_compare_fusion
  7.9 0.7 compare_select_fusion.1
  8.6 0.1 copy.22
  8.7 0.1 copy.23
  8.8 0.1 reshape.242
  9.0 1.7 pad_maximum_fusion
  10.7 3.1 gather_fusion
  13.7 4.5 broadcast_select_fusion
  18.2 0.0 copy-start.5
  18.2 13.3 %all-to-all-start = ((bf16[64,2,128,128]{3,2,1,0:T(8,128)(2,1)}), bf16[64,2,128,128]{3,2,1,0:T(8,128)(2,1)}, u32[]{:S(2)}, u32[]{:S(2)}) async-start(bf16[64,2,128,128]{3,2,1,0:T(8,128)(2,1)} %broadcast_select_fusion), calls=%async_computation | async-start | bytes 8388608 | tf_op jit(solution)/shard_map/all_to_all | solution.py:31
  31.5 0.0 all-gather.2.cloned.1.call-start
  31.6 0.0 copy-done.5
  31.6 95.8 %all-to-all-done = bf16[64,2,128,128]{3,2,1,0:T(8,128)(2,1)} async-done(((bf16[64,2,128,128]{3,2,1,0:T(8,128)(2,1)}), bf16[64,2,128,128]{3,2,1,0:T(8,128)(2,1)}, u32[]{:S(2)}, u32[]{:S(2)}) %all-to-all-start) | async-done | bytes 4194336 | tf_op jit(solution)/shard_map/all_to_all | solution.py:31
  127.4 10.2 %gather_fusion.1 = bf16[192,128,128]{2,1,0:T(8,128)(2,1)} fusion(bf16[128,128,128]{2,1,0:T(8,128)(2,1)} %bitcast.8, s32[1024]{0:T(1024)S(1)} %pad_clamp_fusion), kind=kCustom, calls=%fused_computation.1 | custom fusion | bytes 12583680 | tf_op jit(solution)/shard_map/gather | solution.py:34
  137.7 0.0 copy-start.8
  137.7 0.0 copy-start.9
  137.7 7.4 %bitcast_convert_fusion = bf16[32,128,128]{1,2,0:T(8,128)(2,1)} fusion(bf16[32,6,128,128]{3,2,1,0:T(8,128)(2,1)} %bitcast.75, bf16[32,6,128,128]{3,2,1,0:T(8,128)(2,1)} %bitcast.74), kind=kOutput, calls=%fused_computation.23 | convolution fusion | flops 805830656 | bytes 13631488 | tf_op jit(solution)/shard_map/jpab,jpbc->jac/dot_general | solution.py:36
  145.1 0.0 all-gather.2.cloned.1.call-update
  145.1 0.0 reduce-scatter.2.cloned.1.call-start
  145.2 50.4 %all-gather.2.cloned.1.call-done = bf16[4096,512]{1,0:T(8,128)(2,1)} async-done(((bf16[4096,128]{1,0:T(8,128)(2,1)}), bf16[4096,512]{1,0:T(8,128)(2,1)}) %all-gather.2.cloned.1.call-update) | async-done | bytes 4194320 | tf_op jit(solution)/shard_map/all_gather | solution.py:40
  195.6 0.0 copy-done
  195.6 0.0 copy-done.8
  195.6 0.0 copy-done.9
  195.6 4.5 convert_reduce_fusion
  200.1 4.5 fusion.17
  204.6 0.0 copy-start.7
  204.6 0.0 reduce-scatter.2.cloned.1.call-update
  204.6 0.6 copy-done.7
  205.2 1.9 broadcast.228.clone
  207.1 4.7 scatter_fusion
  211.8 11.5 %all-to-all-start.1 = ((bf16[64,1,128,128]{3,2,1,0:T(8,128)(2,1)}), bf16[64,1,128,128]{3,2,1,0:T(8,128)(2,1)S(1)}, u32[]{:S(2)}, u32[]{:S(2)}) async-start(bf16[64,1,128,128]{3,2,1,0:T(8,128)(2,1)} %bitcast.19), calls=%async_computation.1 | async-start | bytes 4194304 | tf_op jit(solution)/shard_map/all_to_all | solution.py:78
  223.3 66.4 %reduce-scatter.2.cloned.1.call-done = f32[4096,128]{1,0:T(8,128)} async-done(((f32[4096,512]{1,0:T(8,128)}), f32[4096,128]{1,0:T(8,128)}) %reduce-scatter.2.cloned.1.call-update) | async-done | bytes 2097168 | tf_op jit(solution)/shard_map/reduce_scatter | solution.py:67
  289.7 1.7 convert_element_type.30
  291.4 7.3 %fusion.18 = bf16[32,128,6,128]{3,1,2,0:T(8,128)(2,1)} fusion(bf16[32,128,128,1]{2,1,3,0:T(8,128)(2,1)S(1)} %bitcast.83, bf16[32,6,128,128]{3,2,1,0:T(8,128)(2,1)} %bitcast.76), kind=kOutput, calls=%fused_computation.55 | convolution fusion | flops 805306368 | bytes 13631488 | tf_op jit(solution)/shard_map/jpab,jac->jpbc/dot_general | solution.py:71
  298.6 9.1 %copy.26 = bf16[192,128,128]{2,0,1:T(8,128)(2,1)} copy(bf16[192,128,128]{1,2,0:T(8,128)(2,1)} %bitcast.77) | data formatting | bytes 12582912 | tf_op jit(solution)/shard_map/reshape | solution.py:74
  307.7 4.1 convolution_convert_fusion
  311.8 1.4 copy.27
  313.2 1.8 broadcast.228.clone.1
  315.0 5.4 %scatter_fusion.2 = bf16[64,128,128]{2,1,0:T(8,128)(2,1)} fusion(bf16[64,128,128]{2,1,0:T(8,128)(2,1)} %broadcast.228.clone.1, s32[32]{0:T(128)S(1)} %fusion.14, bf16[32,128,128]{2,1,0:T(8,128)(2,1)} %copy.27), kind=kCustom, calls=%fused_computation.4 | custom fusion | bytes 3145856 | tf_op jit(solution)/shard_map/scatter | solution.py:53
  320.4 0.0 all-to-all-done.1
  320.4 0.0 copy-start.4
  320.4 0.0 copy-start.6
  320.4 1.3 copy-done.4
  321.7 10.7 %all-to-all-start.2 = ((bf16[64,1,128,128]{3,2,1,0:T(8,128)(2,1)}), bf16[64,1,128,128]{3,2,1,0:T(8,128)(2,1)}, u32[]{:S(2)}, u32[]{:S(2)}) async-start(bf16[64,1,128,128]{3,2,1,0:T(8,128)(2,1)} %bitcast.30), calls=%async_computation.3 | async-start | bytes 4194304 | tf_op jit(solution)/shard_map/all_to_all | solution.py:79
  332.4 0.0 all-reduce.2.cloned.1.call-start
  332.5 0.0 copy-done.6
  332.5 4.2 fusion.19
  336.7 0.0 all-reduce.2.cloned.1.call-update
  336.7 160.2 %psum.15 = f32[128]{0:T(128)S(1)} all-reduce(f32[128]{0:T(128)S(1)} %get-tuple-element.4), channel_id=1, replica_groups=mesh['dom'=64,'mp'=4] {'dom'}, use_global_device_ids=true, to_apply=%region_7.8 | all-reduce | flops 128 | bytes 1024 | tf_op jit(solution)/shard_map/psum | solution.py:63
  496.9 0.5 broadcast_multiply_fusion.1
  497.4 20.8 %all-reduce.2.cloned.1.call-done = f32[512,128]{1,0:T(8,128)} async-done(((f32[512,128]{1,0:T(8,128)}), f32[512,128]{1,0:T(8,128)}) %all-reduce.2.cloned.1.call-update) | async-done | bytes 262160 | tf_op jit(solution)/shard_map/psum | solution.py:63
  518.3 1.7 broadcast_multiply_fusion
  520.0 0.2 broadcast.212.clone
  520.2 6.7 %scatter_fusion.1 = bf16[32,128,128]{2,1,0:T(8,128)(2,1)S(1)} fusion(bf16[32,128,128]{2,1,0:T(8,128)(2,1)S(1)} %broadcast.212.clone, s32[64]{0:T(128)S(1)} %fusion.15, bf16[64,128,128]{2,1,0:T(8,128)(2,1)} %bitcast.81), kind=kCustom, calls=%fused_computation.3 | custom fusion | bytes 6291712 | tf_op jit(solution)/shard_map/scatter | solution.py:57
  526.9 0.0 copy-start.3
  526.9 0.0 all-to-all-done.2
  526.9 0.0 copy-start.1
  526.9 0.2 broadcast.212.clone.1
  527.1 6.7 %scatter_fusion.3 = bf16[32,128,128]{2,1,0:T(8,128)(2,1)S(1)} fusion(bf16[32,128,128]{2,1,0:T(8,128)(2,1)S(1)} %broadcast.212.clone.1, s32[64]{0:T(128)S(1)} %fusion.15, bf16[64,128,128]{2,1,0:T(8,128)(2,1)} %bitcast.31), kind=kCustom, calls=%fused_computation.5 | custom fusion | bytes 6291712 | tf_op jit(solution)/shard_map/scatter | solution.py:57
  533.8 0.0 copy-done.3
  533.8 0.0 copy-start.2
  533.9 1.0 copy-done.2
  534.8 0.0 copy-done.1
  (5 shorter events, 0.0 us)
Async XLA Ops:
  7.2 188.5 %copy-start = (bf16[512,128]{1,0:T(8,128)(2,1)S(1)}, bf16[512,128]{1,0:T(8,128)(2,1)}, u32[]{:S(2)}) copy-start(bf16[512,128]{1,0:T(8,128)(2,1)} %param.11) | copy-start | bytes 393220
  18.2 13.4 %copy-start.5 = (s32[1,192]{1,0:T(1,128)S(1)}, s32[1,192]{1,0:T(1,128)}, u32[]{:S(2)}) copy-start(s32[1,192]{1,0:T(1,128)} %param.17) | copy-start | bytes 2308
  18.2 109.2 %all-to-all-start = ((bf16[64,2,128,128]{3,2,1,0:T(8,128)(2,1)}), bf16[64,2,128,128]{3,2,1,0:T(8,128)(2,1)}, u32[]{:S(2)}, u32[]{:S(2)}) async-start(bf16[64,2,128,128]{3,2,1,0:T(8,128)(2,1)} %broadcast_select_fusion), calls=%async_computation | async-start | bytes 8388608 | tf_op jit(solution)/shard_map/all_to_all | solution.py:31
  31.5 164.1 %all-gather.2.cloned.1.call-start = ((), (), s32[]{:S(2)}) async-start(), calls=%async_computation.4 | async-start | bytes 5242880 | tf_op jit(solution)/shard_map/all_gather | solution.py:40
  137.7 58.0 %copy-start.8 = (bf16[4096,128]{1,0:T(8,128)(2,1)S(1)}, bf16[4096,128]{1,0:T(8,128)(2,1)}, u32[]{:S(2)}) copy-start(bf16[4096,128]{1,0:T(8,128)(2,1)} %param.13) | copy-start | bytes 3145732
  137.7 58.0 %copy-start.9 = (f32[128]{0:T(128)S(1)}, f32[128]{0:T(128)}, u32[]{:S(2)}) copy-start(f32[128]{0:T(128)} %param.12) | copy-start | bytes 1540
  145.1 144.5 %reduce-scatter.2.cloned.1.call-start = ((), (), s32[]{:S(2)}) async-start(), calls=%async_computation.5 | async-start | bytes 10485760 | tf_op jit(solution)/shard_map/reduce_scatter | solution.py:67
  204.6 0.7 copy-start.7
  211.8 108.6 %all-to-all-start.1 = ((bf16[64,1,128,128]{3,2,1,0:T(8,128)(2,1)}), bf16[64,1,128,128]{3,2,1,0:T(8,128)(2,1)S(1)}, u32[]{:S(2)}, u32[]{:S(2)}) async-start(bf16[64,1,128,128]{3,2,1,0:T(8,128)(2,1)} %bitcast.19), calls=%async_computation.1 | async-start | bytes 4194304 | tf_op jit(solution)/shard_map/all_to_all | solution.py:78
  320.4 1.3 copy-start.4
  320.4 12.1 %copy-start.6 = (s32[1,64,2]{1,2,0:T(2,128)S(1)}, s32[1,64,2]{1,2,0:T(2,128)}, u32[]{:S(2)}) copy-start(s32[1,64,2]{1,2,0:T(2,128)} %param.15) | copy-start | bytes 1540
  321.7 205.2 %all-to-all-start.2 = ((bf16[64,1,128,128]{3,2,1,0:T(8,128)(2,1)}), bf16[64,1,128,128]{3,2,1,0:T(8,128)(2,1)}, u32[]{:S(2)}, u32[]{:S(2)}) async-start(bf16[64,1,128,128]{3,2,1,0:T(8,128)(2,1)} %bitcast.30), calls=%async_computation.3 | async-start | bytes 4194304 | tf_op jit(solution)/shard_map/all_to_all | solution.py:79
  332.4 185.9 %all-reduce.2.cloned.1.call-start = ((), (), s32[]{:S(2)}) async-start(), calls=%async_computation.6 | async-start | bytes 524288 | tf_op jit(solution)/shard_map/psum | solution.py:63
  526.9 7.0 %copy-start.3 = (bf16[32,128,128]{2,1,0:T(8,128)(2,1)}, bf16[32,128,128]{2,1,0:T(8,128)(2,1)S(1)}, u32[]{:S(2)}) copy-start(bf16[32,128,128]{2,1,0:T(8,128)(2,1)S(1)} %scatter_fusion.1) | copy-start | bytes 3145732
  526.9 7.9 %copy-start.1 = (bf16[512,128]{1,0:T(8,128)(2,1)S(1)}, bf16[512,128]{1,0:T(8,128)(2,1)}, u32[]{:S(2)}) copy-start(bf16[512,128]{1,0:T(8,128)(2,1)} %param.11) | copy-start | bytes 393220
  533.8 1.0 copy-start.2
Sparse Core Ops, SparseCore 0:
  145.3 50.3 all-gather.1
  204.7 84.9 reduce-scatter.1
  337.3 180.9 all-reduce.1
where the time goes:
time: 543 us; the launch traced here: 541 us
  waiting for transfers between devices  233 us (43%)
  blocking collectives  160 us (29%)
  local copies, waits for them, and re-layouts  54.6 us (10%)
  starting transfers between devices  35.7 us (7%)
  matrix products  31.9 us (6%)
  between operations  13.9 us (3%)
  other arithmetic  11.5 us (2%)
    psum x1, blocking collectives, on_device(): weight_total, bias_total = lax.psum((weight_part, bias_part), 'dom')  160 us
    all_to_all x1, waiting for transfers between devices, on_device(): lax.all_to_all(outgoing, 'dom', split_axis=0, concat_axis=0, tiled=True)  95.8 us
    reduce_scatter x1, waiting for transfers between devices, on_device(): lax.psum_scatter(partial_terms, 'mp', scatter_dimension=1, tiled=True)  66.4 us
    all_gather x1, waiting for transfers between devices, on_device(): mixed_full = lax.all_gather(mixed_rows, 'mp', axis=1, tiled=True)  50.4 us
    psum x1, waiting for transfers between devices, on_device(): weight_total, bias_total = lax.psum((weight_part, bias_part), 'dom')  20.8 us
    scatter x2, local copies, waits for them, and re-layouts, settle(): empty.at[place_index]  13.4 us
    all_to_all x1, starting transfers between devices, on_device(): lax.all_to_all(outgoing, 'dom', split_axis=0, concat_axis=0, tiled=True)  13.3 us
    all_to_all x1, starting transfers between devices, on_device(): lax.all_to_all(pack_out(fresh_blocks), 'dom', split_axis=0, concat_axis=0...  11.5 us
  transfers between devices with their start and end apart: 6, of which 4 were waited for; matrix products, arithmetic and copies ran while one was open for 9% of the time, Pallas kernels for 0%

commit v1 on v0

v1 whole, which is shorter than its diff:
```python
import functools
import math

import jax
import jax.numpy as jnp
from jax import lax
from jax.experimental import pallas as pl
from jax.experimental.pallas import tpu as pltpu
from jax.sharding import PartitionSpec as P

MESH = pl.DeviceIdType.MESH
CHUNKS = 2
BF16 = jnp.bfloat16
F32 = jnp.float32


def drain(ref, sem):
    pltpu.make_async_copy(ref, ref, sem).wait()


def layer_kernel(
    dims,
    idx,
    bias,
    feat,
    hist,
    weight,
    cot,
    adj,
    fresh_out,
    grad_out,
    wgrad_out,
    bgrad_out,
    tab,
    stage,
    arr,
    adj_v,
    adj_t,
    cotx,
    wx,
    w_full,
    w_t,
    bias_st,
    biasx,
    mixed,
    mixx,
    pg,
    fst,
    fx,
    ast,
    ax,
    rarr,
    cum,
    garr,
    wp,
    wpx,
    ws,
    rsb,
    bsb,
    fin,
    bfin,
    wfin,
    bres,
    loc,
    ysend,
    yrecv,
    zsend,
    zrecv,
):
    n_dom, n_mp, blocks, tpr, blk, col, off = dims
    group = blocks // n_mp
    rows_q = blk // CHUNKS
    tiles = blocks * tpr
    dom = lax.axis_index("dom")
    mp = lax.axis_index("mp")

    def dom_at(i):
        return lax.rem(dom + i, n_dom)

    def mp_at(i):
        return lax.rem(mp + i, n_mp)

    def push(src, dst, send, recv, where):
        pltpu.make_async_remote_copy(
            src_ref=src,
            dst_ref=dst,
            send_sem=send,
            recv_sem=recv,
            device_id=where,
            device_id_type=MESH,
        ).start()

    def over_dom(body):
        lax.fori_loop(1, n_dom, lambda i, c: (body(i), c)[1], 0)

    barrier = pltpu.get_barrier_semaphore()
    for r in range(1, n_mp):
        pl.semaphore_signal(barrier, inc=1, device_id=(dom, mp_at(r)), device_id_type=MESH)
    over_dom(
        lambda i: pl.semaphore_signal(
            barrier, inc=1, device_id=(dom_at(i), mp), device_id_type=MESH
        )
    )
    load_feat = pltpu.make_async_copy(feat, tab.at[pl.ds(0, blocks)], loc.at[0])
    load_hist = pltpu.make_async_copy(hist, tab.at[pl.ds(blocks, blocks)], loc.at[1])
    load_adj = pltpu.make_async_copy(adj, adj_v, loc.at[2])
    own_group = pl.ds(pl.multiple_of(mp * group, group), group)
    load_cot = pltpu.make_async_copy(cot.at[own_group], cotx.at[mp], loc.at[3])
    load_w = pltpu.make_async_copy(weight, wx.at[mp], loc.at[4])
    load_feat.start()
    load_hist.start()
    load_w.start()
    load_cot.start()
    load_adj.start()
    bias_st[...] = jnp.broadcast_to(bias[...], bias_st.shape)
    biasx[mp] = bias_st[...]
    load_feat.wait()
    load_hist.wait()
    pl.semaphore_wait(barrier, n_dom - 1 + n_mp - 1)

    def table_block(d, k):
        return tab[jnp.maximum(idx[off["send"] + 2 * d + k], 0)]

    def send_slots(i):
        d = dom_at(i)
        stage[2 * i] = table_block(d, 0)
        stage[2 * i + 1] = table_block(d, 1)
        push(
            stage.at[pl.ds(2 * i, 2)],
            arr.at[pl.ds(2 * dom, 2)],
            zsend.at[0],
            zrecv.at[0],
            (d, mp),
        )

    over_dom(send_slots)
    arr[2 * dom] = table_block(dom, 0)
    arr[2 * dom + 1] = table_block(dom, 1)

    for r in range(1, n_mp):
        g = mp_at(r)
        theirs = pl.ds(pl.multiple_of(g * group, group), group)
        push(weight, wx.at[mp], ysend.at[0], yrecv.at[0], (dom, g))
        push(bias_st, biasx.at[mp], ysend.at[1], yrecv.at[1], (dom, g))
        push(cot.at[theirs], cotx.at[mp], ysend.at[2], yrecv.at[2], (dom, g))

    load_adj.wait()

    def flip(t, c):
        adj_t[t] = adj_v[t].T
        return c

    lax.fori_loop(0, tiles, flip, 0, unroll=4)

    load_w.wait()
    drain(wx.at[pl.ds(0, n_mp - 1)], yrecv.at[0])
    for m in range(n_mp):
        w_full[:, m * col : (m + 1) * col] = wx[m]
        w_t[m * col : (m + 1) * col, :] = wx[m].T
    drain(biasx.at[pl.ds(0, n_mp - 1)], yrecv.at[1])
    load_cot.wait()
    drain(cotx.at[pl.ds(0, n_mp - 1)], yrecv.at[2])
    bias_row = jnp.concatenate([biasx[m][0:1] for m in range(n_mp)], axis=1)

    drain(stage.at[pl.ds(0, 2 * (n_dom - 1))], zrecv.at[0])

    def mix(q):
        for r in list(range(1, n_mp)) + [0]:
            g = mp_at(r)

            def one(jj, c):
                j = g * group + jj
                left = jnp.concatenate(
                    [adj_v[j * tpr + p, q * rows_q : (q + 1) * rows_q, :] for p in range(tpr)],
                    axis=1,
                )
                right = jnp.concatenate(
                    [arr[idx[off["src"] + j * tpr + p]] for p in range(tpr)], axis=0
                )
                out = jnp.dot(left, right, preferred_element_type=F32).astype(BF16)
                if r:
                    mixed[q, j] = out
                else:
                    mixx[q, mp, jj] = out
                return c

            lax.fori_loop(0, group, one, 0, unroll=2)
            if r:
                theirs = pl.ds(pl.multiple_of(g * group, group), group)
                push(
                    mixed.at[q, theirs],
                    mixx.at[q, mp],
                    ysend.at[3 + q],
                    yrecv.at[3 + q],
                    (dom, g),
                )

    per = 2
    hid = n_mp * col
    root = math.sqrt(2.0 / math.pi)

    def dense(q):
        def one(s, bias_acc):
            b0 = pl.multiple_of(s * per, per)
            x = jnp.concatenate(
                [mixx[q, m, pl.ds(b0, per)].reshape(per * rows_q, col) for m in range(n_mp)],
                axis=1,
            )
            v = jnp.dot(x, w_full[...], preferred_element_type=F32) + bias_row
            square = v * v
            t = jnp.tanh(root * v * (1.0 + 0.044715 * square))
            half = 0.5 * (1.0 + t)
            fresh = (v * half).astype(BF16)
            slope = half + 0.5 * v * (1.0 - t * t) * (root * (1.0 + 3 * 0.044715 * square))
            c = jnp.concatenate(
                [
                    cotx[m, pl.ds(b0, per), q * rows_q : (q + 1) * rows_q, :].reshape(
                        per * rows_q, col
                    )
                    for m in range(n_mp)
                ],
                axis=1,
            )
            p = (c.astype(F32) * slope).astype(BF16)
            pg[q, pl.ds(pl.multiple_of(s * per * rows_q, per * rows_q), per * rows_q), :] = p
            agg = jnp.dot(p, w_t[...], preferred_element_type=F32).astype(BF16)
            for m in range(n_mp):
                cut = slice(m * col, (m + 1) * col)
                fst[q, m, pl.ds(b0, per)] = fresh[:, cut].reshape(per, rows_q, col)
                ast[q, m, pl.ds(b0, per)] = agg[:, cut].reshape(per, rows_q, col)
            return bias_acc + jnp.sum(p.astype(F32).reshape(-1, 8, hid), axis=0)

        total = lax.fori_loop(0, group // per, one, jnp.zeros((8, hid), F32))
        pltpu.make_async_copy(fst.at[q, mp], fx[q].at[own_group], loc.at[5 + q]).start()
        pltpu.make_async_copy(ast.at[q, mp], ax.at[q, own_group], loc.at[5 + CHUNKS + q]).start()
        for r in range(1, n_mp):
            g = mp_at(r)
            push(
                fst.at[q, g],
                fx[q].at[own_group],
                ysend.at[3 + CHUNKS + q],
                yrecv.at[3 + CHUNKS + q],
                (dom, g),
            )
        for r in range(1, n_mp):
            g = mp_at(r)
            push(
                ast.at[q, g],
                ax.at[q, own_group],
                ysend.at[3 + 2 * CHUNKS + q],
                yrecv.at[3 + 2 * CHUNKS + q],
                (dom, g),
            )
        return total

    drain(stage.at[pl.ds(0, 2 * (n_dom - 1))], zsend.at[0])

    def return_fresh(q):
        pltpu.make_async_copy(fst.at[q, mp], fx[q].at[own_group], loc.at[5 + q]).wait()
        drain(fst.at[q, pl.ds(0, n_mp - 1)], yrecv.at[3 + CHUNKS + q])

        def one(i):
            d = dom_at(i)
            stage[i, q * rows_q : (q + 1) * rows_q, :] = fx[q][idx[off["inv"] + d]]
            push(
                stage.at[i, pl.ds(q * rows_q, rows_q)],
                rarr[q].at[dom],
                zsend.at[1 + q],
                zrecv.at[1 + q],
                (d, mp),
            )

        over_dom(one)
        rarr[q][dom] = fx[q][idx[off["inv"] + dom]]

    mix(0)
    bias_acc = jnp.zeros((8, hid), F32)
    for q in range(CHUNKS):
        if q + 1 < CHUNKS:
            mix(q + 1)
        drain(mixx.at[q, pl.ds(0, n_mp - 1)], yrecv.at[3 + q])
        bias_acc = bias_acc + dense(q)
        if q >= 1:
            return_fresh(q - 1)
    return_fresh(CHUNKS - 1)

    for m in range(n_mp):
        part = jnp.zeros((col, hid), F32)
        for q in range(CHUNKS):
            part = part + lax.dot_general(
                mixx[q, m].reshape(group * rows_q, col),
                pg[q],
                (((0,), (0,)), ((), ())),
                preferred_element_type=F32,
            )
        for m2 in range(n_mp):
            wp[m2, m * (col // 8) : (m + 1) * (col // 8)] = part[
                :, m2 * col : (m2 + 1) * col
            ].reshape(col // 8, 8, col)
    for m in range(n_mp):
        wp[m, hid // 8] = bias_acc[:, m * col : (m + 1) * col]
    for r in range(1, n_mp):
        g = mp_at(r)
        push(wp.at[g], wpx.at[mp], ysend.at[3 + 3 * CHUNKS], yrecv.at[3 + 3 * CHUNKS], (dom, g))
    wpx[mp] = wp[mp]

    for q in range(CHUNKS):
        pltpu.make_async_copy(
            ast.at[q, mp], ax.at[q, own_group], loc.at[5 + CHUNKS + q]
        ).wait()
        drain(ast.at[q, pl.ds(0, n_mp - 1)], yrecv.at[3 + 2 * CHUNKS + q])

    step = 8

    def back(s, acc):
        terms = []
        for u in range(step):
            i = s * step + u
            t = idx[off["order"] + i]
            b = idx[off["block"] + i]
            rows = jnp.concatenate([ax[q, b] for q in range(CHUNKS)], axis=0)
            terms.append(jnp.dot(adj_t[t], rows, preferred_element_type=F32))
        for u in range(step):
            i = s * step + u
            acc = jnp.where(idx[off["new"] + i] > 0, terms[u], acc + terms[u])
            cum[i] = acc.astype(BF16)
        return acc

    lax.fori_loop(0, tiles // step, back, jnp.zeros((blk, col), F32))

    drain(wp.at[pl.ds(0, n_mp - 1)], yrecv.at[3 + 3 * CHUNKS])
    chunks = hid // 8
    total = wpx[0]
    for m in range(1, n_mp):
        total = total + wpx[m]
    ws[...] = total

    def send_rows(i):
        d = dom_at(i)
        push(ws.at[d], rsb.at[dom], zsend.at[1 + CHUNKS], zrecv.at[1 + CHUNKS], (d, mp))

    over_dom(send_rows)
    rsb[dom] = ws[dom]

    @pl.when(dom != 0)
    def _():
        push(ws.at[chunks], bsb.at[dom], zsend.at[2 + CHUNKS], zrecv.at[2 + CHUNKS], (0, mp))

    def grad_block(d):
        at = idx[off["end"] + d]
        found = cum[jnp.maximum(at, 0)]
        return jnp.where(at >= 0, found, jnp.zeros_like(found))

    def send_grad(i):
        d = dom_at(i)
        stage[n_dom + i] = grad_block(d)
        push(stage.at[n_dom + i], garr.at[dom], zsend.at[3 + CHUNKS], zrecv.at[3 + CHUNKS], (d, mp))

    over_dom(send_grad)
    garr[dom] = grad_block(dom)

    drain(rsb.at[pl.ds(0, n_dom - 1)], zrecv.at[1 + CHUNKS])
    fin[...] = jnp.sum(rsb[...], axis=0) * (1.0 / n_dom)
    over_dom(
        lambda i: push(fin, wfin.at[dom], zsend.at[4 + CHUNKS], zrecv.at[4 + CHUNKS], (dom_at(i), mp))
    )
    wfin[dom] = fin[...]

    @pl.when(dom == 0)
    def _():
        bsb[0] = ws[chunks]
        drain(bsb.at[pl.ds(0, n_dom - 1)], zrecv.at[2 + CHUNKS])
        line = jnp.sum(jnp.sum(bsb[...], axis=0), axis=0, keepdims=True) * (1.0 / n_dom)
        bfin[...] = jnp.broadcast_to(line, bfin.shape)
        over_dom(
            lambda i: push(bfin, bres, zsend.at[5 + CHUNKS], zrecv.at[5 + CHUNKS], (dom_at(i), mp))
        )
        bgrad_out[...] = line

    for q in range(CHUNKS):
        drain(rarr[q].at[pl.ds(0, n_dom - 1)], zrecv.at[1 + q])

        def settle(j, c):
            fresh_out[j, q * rows_q : (q + 1) * rows_q, :] = rarr[q][idx[off["rev"] + j]]
            return c

        lax.fori_loop(0, blocks, settle, 0, unroll=2)

    @pl.when(dom != 0)
    def _():
        drain(bres, zrecv.at[5 + CHUNKS])
        bgrad_out[...] = bres[0:1]

    drain(wfin.at[pl.ds(0, n_dom - 1)], zrecv.at[4 + CHUNKS])
    wgrad_out[...] = wfin[...]
    drain(garr.at[pl.ds(0, n_dom - 1)], zrecv.at[3 + CHUNKS])

    def settle_grad(j, c):
        grad_out[j] = garr[idx[off["rev"] + j]]
        return c

    lax.fori_loop(0, blocks, settle_grad, 0, unroll=2)

    peers = pl.ds(0, n_mp - 1)
    others = pl.ds(0, n_dom - 1)
    drain(wx.at[peers], ysend.at[0])
    drain(biasx.at[peers], ysend.at[1])
    drain(cotx.at[peers], ysend.at[2])
    for q in range(CHUNKS):
        drain(mixx.at[q, peers], ysend.at[3 + q])
        drain(fst.at[q, peers], ysend.at[3 + CHUNKS + q])
        drain(ast.at[q, peers], ysend.at[3 + 2 * CHUNKS + q])
        drain(rarr[q].at[others], zsend.at[1 + q])
    drain(wp.at[peers], ysend.at[3 + 3 * CHUNKS])
    drain(rsb.at[others], zsend.at[1 + CHUNKS])
    drain(garr.at[others], zsend.at[3 + CHUNKS])
    drain(wfin.at[others], zsend.at[4 + CHUNKS])

    @pl.when(dom != 0)
    def _():
        drain(ws.at[chunks], zsend.at[2 + CHUNKS])

    @pl.when(dom == 0)
    def _():
        drain(bsb.at[others], zsend.at[5 + CHUNKS])


def on_device(
    features, history, weight, bias_vector, cotangent, adj_tiles, send_list, batch_slot, tile_src
):
    n_dom = lax.axis_size("dom")
    n_mp = lax.axis_size("mp")
    blk = adj_tiles.shape[1]
    col = features.shape[1]
    blocks = features.shape[0] // blk
    tiles = tile_src.shape[1]
    tpr = tiles // blocks
    hid = n_mp * col
    group = blocks // n_mp
    rows_q = blk // CHUNKS

    wanted = send_list[0]
    slots = batch_slot[0]
    src = tile_src[0]
    ids = jnp.arange(blocks, dtype=jnp.int32)
    doms = jnp.arange(n_dom, dtype=jnp.int32)
    ts = jnp.arange(tiles, dtype=jnp.int32)
    owner = slots // 2
    inverse = jnp.sum(jnp.where(owner[None, :] == doms[:, None], ids[None, :], 0), axis=1)
    reverse = jnp.sum(jnp.where(wanted[:, 0][None, :] == ids[:, None], doms[None, :], 0), axis=1)
    hit = src[:, None] == slots[None, :]
    target = blocks - jnp.sum(jnp.where(hit, blocks - ids[None, :], 0), axis=1)
    key = target * tiles + ts
    rank = jnp.sum((key[None, :] < key[:, None]).astype(jnp.int32), axis=1)
    place = rank[None, :] == ts[:, None]
    order = jnp.sum(jnp.where(place, ts[None, :], 0), axis=1)
    count = jnp.sum(hit.astype(jnp.int32), axis=0)
    upto = jnp.sum((target[:, None] <= ids[None, :]).astype(jnp.int32), axis=0)
    begin = upto - count
    new = jnp.sum(
        jnp.where((begin[None, :] == ts[:, None]) & (count > 0)[None, :], 1, 0), axis=1
    ) + (ts == upto[-1])
    last = jnp.where(count > 0, upto - 1, -1)
    last_of = jnp.sum(
        jnp.where(owner[None, :] == doms[:, None], last[None, :] + 1, 0), axis=1
    ) - 1
    pieces = [
        ("send", wanted.reshape(-1)),
        ("src", src),
        ("inv", inverse),
        ("rev", reverse),
        ("order", order),
        ("block", order // tpr),
        ("new", new),
        ("end", last_of),
    ]
    off, at = {}, 0
    for name, piece in pieces:
        off[name] = at
        at += piece.shape[0]
    idx = jnp.concatenate([piece.astype(jnp.int32) for _, piece in pieces])

    vm = pltpu.VMEM
    scratch = [
        vm((2 * blocks, blk, col), BF16),
        vm((2 * n_dom, blk, col), BF16),
        vm((2 * n_dom, blk, col), BF16),
        vm((tiles, blk, blk), BF16),
        vm((tiles, blk, blk), BF16),
        vm((n_mp, group, blk, col), BF16),
        vm((n_mp, hid, col), BF16),
        vm((hid, hid), BF16),
        vm((hid, hid), BF16),
        vm((8, col), F32),
        vm((n_mp, 8, col), F32),
        vm((CHUNKS, blocks, rows_q, col), BF16),
        vm((CHUNKS, n_mp, group, rows_q, col), BF16),
        vm((CHUNKS, group * rows_q, hid), BF16),
        vm((CHUNKS, n_mp, group, rows_q, col), BF16),
        tuple(vm((blocks, rows_q, col), BF16) for _ in range(CHUNKS)),
        vm((CHUNKS, n_mp, group, rows_q, col), BF16),
        vm((CHUNKS, blocks, rows_q, col), BF16),
        tuple(vm((n_dom, rows_q, col), BF16) for _ in range(CHUNKS)),
        vm((tiles, blk, col), BF16),
        vm((n_dom, blk, col), BF16),
        vm((n_mp, hid // 8 + 1, 8, col), F32),
        vm((n_mp, hid // 8 + 1, 8, col), F32),
        vm((hid // 8 + 1, 8, col), F32),
        vm((n_dom, 8, col), F32),
        vm((n_dom, 8, col), F32),
        vm((8, col), F32),
        vm((8, col), F32),
        vm((n_dom, 8, col), F32),
        vm((8, col), F32),
        pltpu.SemaphoreType.DMA((5 + 2 * CHUNKS,)),
        pltpu.SemaphoreType.DMA((4 + 3 * CHUNKS,)),
        pltpu.SemaphoreType.DMA((4 + 3 * CHUNKS,)),
        pltpu.SemaphoreType.DMA((6 + CHUNKS,)),
        pltpu.SemaphoreType.DMA((6 + CHUNKS,)),
    ]
    in_vmem = pl.BlockSpec(memory_space=pltpu.VMEM)
    anywhere = pl.BlockSpec(memory_space=pl.ANY)
    dims = (n_dom, n_mp, blocks, tpr, blk, col, off)
    fresh, grad, wgrad, bgrad = pl.pallas_call(
        functools.partial(layer_kernel, dims),
        name="layer",
        out_shape=(
            jax.ShapeDtypeStruct((blocks, blk, col), BF16),
            jax.ShapeDtypeStruct((blocks, blk, col), BF16),
            jax.ShapeDtypeStruct((n_dom, 8, col), F32),
            jax.ShapeDtypeStruct((1, col), F32),
        ),
        in_specs=[pl.BlockSpec(memory_space=pltpu.SMEM), in_vmem] + [anywhere] * 5,
        out_specs=(in_vmem,) * 4,
        scratch_shapes=scratch,
        compiler_params=pltpu.CompilerParams(
            collective_id=1, has_side_effects=True, vmem_limit_bytes=60 * 1024 * 1024
        ),
    )(
        idx,
        bias_vector.reshape(1, col),
        features.reshape(blocks, blk, col),
        history.reshape(blocks, blk, col),
        weight,
        cotangent.reshape(blocks, blk, col),
        adj_tiles,
    )
    return (
        fresh.reshape(blocks * blk, col),
        grad.reshape(blocks * blk, col),
        wgrad.reshape(hid, col),
        bgrad.reshape(col),
    )


def solution(mesh):
    placed = (
        P("dom", "mp"),
        P("dom", "mp"),
        P(None, "mp"),
        P("mp"),
        P("dom", "mp"),
        P("dom", None, None),
        P("dom", None, None),
        P("dom", None),
        P("dom", None),
    )
    return jax.shard_map(
        on_device,
        mesh=mesh,
        in_specs=placed,
        out_specs=(P("dom", "mp"), P("dom", "mp"), P(None, "mp"), P("mp")),
        check_vma=False,
    )
```

time: 543 us -> 253 us (0.47)
  Pallas kernels: 0 us -> 238 us
  waiting for transfers between devices: 233 us -> 0 us
  blocking collectives: 160 us -> 0 us
  local copies, waits for them, and re-layouts: 54.6 us -> 10.8 us
  starting transfers between devices: 35.7 us -> 0 us
  matrix products: 31.9 us -> 0 us
  between operations: 13.9 us -> 0.67 us
  other arithmetic: 11.5 us -> 2.96 us
    pallas_call x0 -> x1, Pallas kernels: none -> 238 us  [on_device(): pl.pallas_call(functools.partial(layer_kernel, dims), name='layer', out_s...]
    psum x1 -> x0, blocking collectives: 160 us -> none  [on_device(): weight_total, bias_total = lax.psum((weight_part, bias_part), 'dom')]
    all_to_all x3 -> x0, waiting for transfers between devices: 95.8 us -> none  [the longest x1 95.8 us: on_device(): lax.all_to_all(outgoing, 'dom', split_axis=0, concat_axis=0, tiled=True)]
    reduce_scatter x1 -> x0, waiting for transfers between devices: 66.4 us -> none  [on_device(): lax.psum_scatter(partial_terms, 'mp', scatter_dimension=1, tiled=True)]
    all_gather x1 -> x0, waiting for transfers between devices: 50.4 us -> none  [on_device(): mixed_full = lax.all_gather(mixed_rows, 'mp', axis=1, tiled=True)]
    all_to_all x3 -> x0, starting transfers between devices: 35.5 us -> none  [the longest x1 13.3 us: on_device(): lax.all_to_all(outgoing, 'dom', split_axis=0, concat_axis=0, tiled=True)]
    dot_general x6 -> x0, matrix products: 31.9 us -> none  [the longest x1 7.45 us: on_device(): jnp.einsum('jpab,jpbc->jac', tile_vals, gathered, preferred_element_type=...]
    scatter x4 -> x0, local copies, waits for them, and re-layouts: 23.4 us -> none  [the longest x2 13.4 us: settle(): empty.at[place_index]]
  transfers between devices with their start and end apart: 6 -> 0, of which waited for: 4 -> 0; matrix products, arithmetic and copies ran while one was open for 9% -> 0% of each run, Pallas kernels for 0% -> 0%
where the time goes in v1:
time: 253 us
  Pallas kernels  238 us (94%)
  local copies, waits for them, and re-layouts  10.8 us (4%)
  other arithmetic  2.96 us (1%)
    pallas_call x1, Pallas kernels, on_device(): pl.pallas_call(functools.partial(layer_kernel, dims), name='layer', out_s...  238 us
    unnamed x5, local copies, waits for them, and re-layouts  8.07 us

profile of v1, /device:TPU:1, one launch (start us, length us, event | category | flops | bytes accessed | tf_op | source)
XLA Modules:
  0.0 252.7 jit_solution(10773411438049004831)
XLA Ops:
  0.6 0.7 slice_bitcast_fusion
  1.3 0.1 select_reduce_fusion.3
  1.4 0.7 fusion.4
  2.1 0.9 fusion.1
  3.0 0.2 convert_reduce_fusion
  3.2 0.1 select_reduce_fusion
  3.3 0.1 convert_reduce_fusion.1
  3.4 0.6 slice.7
  4.0 0.1 select_reduce_fusion.1
  4.1 0.7 and_select_fusion
  4.8 0.1 select_reduce_fusion.2
  4.9 0.8 copy.15
  5.7 0.1 reshape_squeeze.3
  5.8 1.4 concatenate.3.idx
  7.2 238.3 %layer.1 = (bf16[32,128,128]{2,1,0:T(8,128)(2,1)}, bf16[32,128,128]{2,1,0:T(8,128)(2,1)}, f32[64,8,128]{2,1,0:T(8,128)}, f32[1,128]{1,0:T(1,128)}) custom-call(s32[1056]{0:T(1024)} %concatenate.3.idx, f32[1,128]{1,0:T(1,128)} %bitcast.25, bf16[32,128,128]{2,1,0:T(8,128)(2,1)} %bitcast.18, bf16[32,128,128]{2,1,0:T(8,128)(2,1)} %bitcast.19, ...), custom_call_target="tpu_custom_call" | custom-call | tf_op jit(solution)/shard_map/layer/pallas_call | solution.py:524
  245.4 2.3 copy.20
  247.7 2.3 copy.21
  249.9 1.7 copy.22
  251.6 1.1 copy.23
  (5 shorter events, 0.0 us)
